TPU v7x, 32 devices: a whole 2x2x4 slice. The times are simulated.
32 devices in a mesh: row: 8 (over z, x), col: 4 (over y, core).
Axes of the slice: x: 2, y: 2, z: 4, core: 2. Of those that a mesh axis runs over, the one named last changes fastest.
Arguments:
- start_block: float32 [16, 73728], P(None, ('row', 'col'))
- start_search: float32 [16, 73728], P(None, ('row', 'col')), may hold values from -6 to 6
- precond: float32 [73728], P(('row', 'col')), may hold values from 0.25 to 1
- diag_energy: float32 [73728], P(('row', 'col')), may hold values from 1 to 16
- blocks: bfloat16 [8, 4, 64, 128, 128], P('row', 'col'), may hold values from -0.375 to 0.375
- row_index: int32 [8, 4, 64], P('row', 'col'), may hold values from 0 to 71
- col_index: int32 [8, 4, 64], P('row', 'col'), may hold values from 0 to 143
- live_count: int32 [8, 4], P('row', 'col'), may hold values from 16 to 64, as said below
- ritz_coeffs: float32 [2, 3, 16, 16], replicated
Outputs:
- final_block: float32 [16, 73728], P(None, ('row', 'col'))
- ritz_values: float32 [16], replicated
Inputs may be any that keep to these rules, and one draw needn't show every extreme that they name: Every live_count is at least 16, and some device has all 64 slots live.
All inputs are finite; a program needn't handle non-finite values.
Results may differ from a plain program's by a relative error of at most 0.019.
Values may be sent and summed in bfloat16 or wider, within the bound.
A program may use at most 64 MiB of HBM per device.

v0:
```python
import jax
import jax.numpy as jnp
from jax import lax
from jax.sharding import PartitionSpec as P

ITERS = 2


def slot_terms(tile_set, row_ids, col_ids, alive, col_tiles, row_tiles):
    slots = tile_set.shape[0]
    gathered_col = jnp.take(col_tiles, col_ids, axis=0)
    gathered_row = jnp.take(row_tiles, row_ids, axis=0)
    direct = jnp.einsum("bij,bkj->bki", tile_set, gathered_col, preferred_element_type=jnp.float32)
    transposed = jnp.einsum(
        "bij,bki->bkj", tile_set, gathered_row, preferred_element_type=jnp.float32
    )
    nrows = row_tiles.shape[0]
    ncols = col_tiles.shape[0]
    hot_rows = ((jnp.arange(nrows)[:, None] == row_ids[None, :]) & alive[None, :]).astype(
        jnp.float32
    )
    hot_cols = ((jnp.arange(ncols)[:, None] == col_ids[None, :]) & alive[None, :]).astype(
        jnp.float32
    )
    row_total = jnp.dot(hot_rows, direct.reshape(slots, -1), precision=lax.Precision.HIGHEST)
    col_total = jnp.dot(hot_cols, transposed.reshape(slots, -1), precision=lax.Precision.HIGHEST)
    return (row_total, col_total)


def apply_operator(vec_bf, diag_energy, blocks, row_index, col_index, live_count):
    vec_count = vec_bf.shape[0]
    block_size = blocks.shape[-1]
    tile_set = blocks[0, 0]
    row_ids = row_index[0, 0]
    col_ids = col_index[0, 0]
    live = live_count[0, 0]
    slots = tile_set.shape[0]
    col_vec = lax.all_gather(vec_bf, "row", axis=1, tiled=True)
    row_vec = lax.all_gather(vec_bf, "col", axis=1, tiled=True)
    col_tiles = col_vec.reshape(vec_count, -1, block_size).transpose(1, 0, 2)
    row_tiles = row_vec.reshape(vec_count, -1, block_size).transpose(1, 0, 2)
    nrows = row_tiles.shape[0]
    ncols = col_tiles.shape[0]
    alive = jnp.arange(slots) < live
    row_total, col_total = slot_terms(tile_set, row_ids, col_ids, alive, col_tiles, row_tiles)
    direct_sum = (
        row_total.reshape(nrows, vec_count, block_size).transpose(1, 0, 2).reshape(vec_count, -1)
    )
    trans_sum = (
        col_total.reshape(ncols, vec_count, block_size).transpose(1, 0, 2).reshape(vec_count, -1)
    )
    direct_sum = lax.psum_scatter(direct_sum, "col", scatter_dimension=1, tiled=True)
    trans_sum = lax.psum_scatter(trans_sum, "row", scatter_dimension=1, tiled=True)
    return direct_sum + trans_sum + diag_energy[None, :] * vec_bf.astype(jnp.float32)


def quotients(block, image):
    numerator, denominator = lax.psum(
        (jnp.sum(block * image, axis=1), jnp.sum(block * block, axis=1)), ("row", "col")
    )
    return numerator / denominator


def combine_three(coef_a, first, coef_b, second, coef_c, third):
    hi = lax.Precision.HIGHEST
    return (
        jnp.dot(coef_a.T, first, precision=hi)
        + jnp.dot(coef_b.T, second, precision=hi)
        + jnp.dot(coef_c.T, third, precision=hi)
    )


def on_device(
    start_block,
    start_search,
    precond,
    diag_energy,
    blocks,
    row_index,
    col_index,
    live_count,
    ritz_coeffs,
):
    hi = lax.Precision.HIGHEST
    block = start_block
    search = start_search
    block_bf = block.astype(jnp.bfloat16)
    search_bf = search.astype(jnp.bfloat16)
    image_x = apply_operator(block_bf, diag_energy, blocks, row_index, col_index, live_count)
    image_p = apply_operator(search_bf, diag_energy, blocks, row_index, col_index, live_count)
    for iteration in range(ITERS):
        ritz_now = quotients(block, image_x)
        residual = (image_x - ritz_now[:, None] * block) * precond[None, :]
        image_r = apply_operator(
            residual.astype(jnp.bfloat16), diag_energy, blocks, row_index, col_index, live_count
        )
        coef_x = ritz_coeffs[iteration, 0]
        coef_w = ritz_coeffs[iteration, 1]
        coef_p = ritz_coeffs[iteration, 2]
        new_block = combine_three(coef_x, block, coef_w, residual, coef_p, search)
        new_search = jnp.dot(coef_w.T, residual, precision=hi) + jnp.dot(
            coef_p.T, search, precision=hi
        )
        new_image_x = combine_three(coef_x, image_x, coef_w, image_r, coef_p, image_p)
        new_image_p = jnp.dot(coef_w.T, image_r, precision=hi) + jnp.dot(
            coef_p.T, image_p, precision=hi
        )
        block, search, image_x, image_p = (new_block, new_search, new_image_x, new_image_p)
    return (block, quotients(block, image_x))


def solution(mesh):
    placed = (
        P(None, ("row", "col")),
        P(None, ("row", "col")),
        P(("row", "col")),
        P(("row", "col")),
        P("row", "col", None, None, None),
        P("row", "col", None),
        P("row", "col", None),
        P("row", "col"),
        P(),
    )
    return jax.shard_map(
        on_device,
        mesh=mesh,
        in_specs=placed,
        out_specs=(P(None, ("row", "col")), P()),
        check_vma=False,
    )
```

profile of v0, /device:TPU:0, one launch (start us, length us, event | category | flops | bytes accessed | tf_op | source)
XLA Modules:
  0.0 538.5 jit_solution(15913298779357787468)
XLA Ops:
  10.3 33.2 %all_gather.24 = bf16[16,18432]{1,0:T(8,128)(2,1)S(1)} all-gather(bf16[16,2304]{1,0:T(8,128)(2,1)S(1)} %convert_element_type.32), channel_id=1, replica_groups=mesh['row'=8,'col'=4] {'row'}, dimensions={1}, use_global_device_ids=true | all-gather | bytes 663552 | tf_op jit(solution)/shard_map/all_gather | solution.py:38
  44.2 1.2 fusion.20
  47.1 5.9 %all_gather.25 = bf16[16,9216]{1,0:T(8,128)(2,1)S(1)} all-gather(bf16[16,2304]{1,0:T(8,128)(2,1)S(1)} %convert_element_type.32), channel_id=1, replica_groups=mesh['row'=8,'col'=4] {'col'}, dimensions={1}, use_global_device_ids=true | all-gather | bytes 368640 | tf_op jit(solution)/shard_map/all_gather | solution.py:39
  55.3 1.4 copy.134
  56.8 32.5 %all_gather.28 = bf16[16,18432]{1,0:T(8,128)(2,1)S(1)} all-gather(bf16[16,2304]{1,0:T(8,128)(2,1)S(1)} %convert_element_type.36), channel_id=1, replica_groups=mesh['row'=8,'col'=4] {'row'}, dimensions={1}, use_global_device_ids=true | all-gather | bytes 663552 | tf_op jit(solution)/shard_map/all_gather | solution.py:38
  90.0 1.2 fusion.12
  92.9 5.9 %all_gather.29 = bf16[16,9216]{1,0:T(8,128)(2,1)S(1)} all-gather(bf16[16,2304]{1,0:T(8,128)(2,1)S(1)} %convert_element_type.36), channel_id=1, replica_groups=mesh['row'=8,'col'=4] {'col'}, dimensions={1}, use_global_device_ids=true | all-gather | bytes 368640 | tf_op jit(solution)/shard_map/all_gather | solution.py:39
  101.0 1.4 copy.132
  102.5 35.4 %reduce-scatter.11.cloned.1.call-done = f32[16,2304]{1,0:T(8,128)} async-done(((f32[16,18432]{1,0:T(8,128)}), f32[16,2304]{1,0:T(8,128)}) %reduce-scatter.11.cloned.1.call-update) | async-done | bytes 147472 | tf_op jit(solution)/shard_map/reduce_scatter | solution.py:53
  139.0 39.9 %all-reduce.2 = (f32[16]{0:T(128)S(1)}, f32[16]{0:T(128)S(1)}) all-reduce(f32[16]{0:T(128)S(1)} %get-tuple-element.7, f32[16]{0:T(128)S(1)} %get-tuple-element.6), channel_id=1, replica_groups=mesh['row'=8,'col'=4] {'row','col'}, use_global_device_ids=true, to_apply=%region_3.6 | all-reduce | flops 32 | bytes 256 | tf_op jit(solution)/shard_map/psum | solution.py:58
  179.0 1.7 fusion.137
  180.7 32.6 %all_gather.26 = bf16[16,18432]{1,0:T(8,128)(2,1)S(1)} all-gather(bf16[16,2304]{1,0:T(8,128)(2,1)S(1)} %get-tuple-element.14), channel_id=1, replica_groups=mesh['row'=8,'col'=4] {'row'}, dimensions={1}, use_global_device_ids=true | all-gather | bytes 663552 | tf_op jit(solution)/shard_map/all_gather | solution.py:38
  214.0 1.2 fusion.16
  216.9 6.5 %all_gather.27 = bf16[16,9216]{1,0:T(8,128)(2,1)S(1)} all-gather(bf16[16,2304]{1,0:T(8,128)(2,1)S(1)} %get-tuple-element.14), channel_id=1, replica_groups=mesh['row'=8,'col'=4] {'col'}, dimensions={1}, use_global_device_ids=true | all-gather | bytes 368640 | tf_op jit(solution)/shard_map/all_gather | solution.py:39
  225.6 1.4 copy.133
  227.8 2.3 reduce-scatter.19.cloned.1.call-done
  230.1 1.3 convolution_bitcast_fusion
  231.4 22.1 %reduce-scatter.13.cloned.1.call-done = f32[16,2304]{1,0:T(8,128)} async-done(((f32[16,9216]{1,0:T(8,128)}), f32[16,2304]{1,0:T(8,128)}) %reduce-scatter.13.cloned.1.call-update) | async-done | bytes 147472 | tf_op jit(solution)/shard_map/reduce_scatter | solution.py:52
  253.6 67.3 %reduce-scatter.15.cloned.1.call-done = f32[16,2304]{1,0:T(8,128)} async-done(((f32[16,18432]{1,0:T(8,128)}), f32[16,2304]{1,0:T(8,128)}) %reduce-scatter.15.cloned.1.call-update) | async-done | bytes 147472 | tf_op jit(solution)/shard_map/reduce_scatter | solution.py:53
  320.9 1.3 convolution_bitcast_fusion.1
  323.0 39.9 %all-reduce.1 = (f32[16]{0:T(128)S(1)}, f32[16]{0:T(128)S(1)}) all-reduce(f32[16]{0:T(128)S(1)} %get-tuple-element.5, f32[16]{0:T(128)S(1)} %get-tuple-element.4), channel_id=1, replica_groups=mesh['row'=8,'col'=4] {'row','col'}, use_global_device_ids=true, to_apply=%region_11.14 | all-reduce | flops 32 | bytes 256 | tf_op jit(solution)/shard_map/psum | solution.py:58
  363.1 31.5 %all_gather.30 = bf16[16,18432]{1,0:T(8,128)(2,1)S(1)} all-gather(bf16[16,2304]{1,0:T(8,128)(2,1)S(1)} %fusion.124), channel_id=1, replica_groups=mesh['row'=8,'col'=4] {'row'}, dimensions={1}, use_global_device_ids=true | all-gather | bytes 663552 | tf_op jit(solution)/shard_map/all_gather | solution.py:38
  395.4 1.7 gather_fusion.6
  397.1 1.2 fusion.8
  400.0 6.8 %all_gather.31 = bf16[16,9216]{1,0:T(8,128)(2,1)S(1)} all-gather(bf16[16,2304]{1,0:T(8,128)(2,1)S(1)} %fusion.124), channel_id=1, replica_groups=mesh['row'=8,'col'=4] {'col'}, dimensions={1}, use_global_device_ids=true | all-gather | bytes 368640 | tf_op jit(solution)/shard_map/all_gather | solution.py:39
  406.9 1.3 gather_fusion.7
  408.2 1.6 fusion.6
  410.6 1.4 copy.131
  413.5 8.0 %reduce-scatter.21.cloned.1.call-done = f32[16,2304]{1,0:T(8,128)} async-done(((f32[16,9216]{1,0:T(8,128)}), f32[16,2304]{1,0:T(8,128)}) %reduce-scatter.21.cloned.1.call-update) | async-done | bytes 147472 | tf_op jit(solution)/shard_map/reduce_scatter | solution.py:52
  421.5 67.9 %reduce-scatter.23.cloned.1.call-done = f32[16,2304]{1,0:T(8,128)} async-done(((f32[16,18432]{1,0:T(8,128)}), f32[16,2304]{1,0:T(8,128)}) %reduce-scatter.23.cloned.1.call-update) | async-done | bytes 147472 | tf_op jit(solution)/shard_map/reduce_scatter | solution.py:53
  489.4 1.3 convolution_add_fusion.1
  491.1 40.0 %all-reduce = (f32[16]{0:T(128)S(1)}, f32[16]{0:T(128)S(1)}) all-reduce(f32[16]{0:T(128)S(1)} %fusion.22, f32[16]{0:T(128)S(1)} %get-tuple-element.17), channel_id=1, replica_groups=mesh['row'=8,'col'=4] {'row','col'}, use_global_device_ids=true, to_apply=%region_17.20 | all-reduce | flops 32 | bytes 256 | tf_op jit(solution)/shard_map/psum | solution.py:58
  (94 shorter events, 24.8 us)
Async XLA Ops:
  7.2 37.1 %copy-start = (bf16[1,1,64,128,128]{4,3,2,1,0:T(8,128)(2,1)S(1)}, bf16[1,1,64,128,128]{4,3,2,1,0:T(8,128)(2,1)}, u32[]{:S(2)}) copy-start(bf16[1,1,64,128,128]{4,3,2,1,0:T(8,128)(2,1)} %param.17) | copy-start | bytes 6291460
  7.2 95.3 %reduce-scatter.9.cloned.1.call-start = ((), (), s32[]{:S(2)}) async-start(), calls=%async_computation.8 | async-start | bytes 737280 | tf_op jit(solution)/shard_map/reduce_scatter | solution.py:52
  43.5 2.0 copy-start.10
  47.1 90.8 %reduce-scatter.11.cloned.1.call-start = ((), (), s32[]{:S(2)}) async-start(), calls=%async_computation.9 | async-start | bytes 1327104 | tf_op jit(solution)/shard_map/reduce_scatter | solution.py:53
  47.1 7.4 %copy-start.11 = (s32[1,1,64]{2,1,0:T(1,128)S(1)}, s32[1,1,64]{2,1,0:T(1,128)}, u32[]{:S(2)}) copy-start(s32[1,1,64]{2,1,0:T(1,128)} %param.19) | copy-start | bytes 772
  55.3 1.5 copy-start.4
  56.7 171.1 %reduce-scatter.17.cloned.1.call-start = ((), (), s32[]{:S(2)}) async-start(), calls=%async_computation.12 | async-start | bytes 737280 | tf_op jit(solution)/shard_map/reduce_scatter | solution.py:52
  92.9 137.3 %reduce-scatter.19.cloned.1.call-start = ((), (), s32[]{:S(2)}) async-start(), calls=%async_computation.13 | async-start | bytes 1327104 | tf_op jit(solution)/shard_map/reduce_scatter | solution.py:53
  101.0 36.9 %copy-start.1 = (f32[16,2304]{1,0:T(8,128)S(1)}, f32[16,2304]{1,0:T(8,128)}, u32[]{:S(2)}) copy-start(f32[16,2304]{1,0:T(8,128)} %param.13) | copy-start | bytes 442372
  101.0 36.9 %copy-start.7 = (f32[2304]{0:T(1024)S(1)}, f32[2304]{0:T(1024)}, u32[]{:S(2)}) copy-start(f32[2304]{0:T(1024)} %param.16) | copy-start | bytes 27652
  101.0 78.0 %copy-start.9 = (f32[2304]{0:T(1024)S(1)}, f32[2304]{0:T(1024)}, u32[]{:S(2)}) copy-start(f32[2304]{0:T(1024)} %param.15) | copy-start | bytes 27652
  102.4 151.1 %reduce-scatter.13.cloned.1.call-start = ((), (), s32[]{:S(2)}) async-start(), calls=%async_computation.10 | async-start | bytes 737280 | tf_op jit(solution)/shard_map/reduce_scatter | solution.py:52
  216.8 104.1 %reduce-scatter.15.cloned.1.call-start = ((), (), s32[]{:S(2)}) async-start(), calls=%async_computation.11 | async-start | bytes 1327104 | tf_op jit(solution)/shard_map/reduce_scatter | solution.py:53
  225.6 1.5 copy-start.8
  225.6 1.9 copy-start.5
  225.6 96.6 %copy-start.2 = (f32[16,2304]{1,0:T(8,128)S(1)}, f32[16,2304]{1,0:T(8,128)}, u32[]{:S(2)}) copy-start(f32[16,2304]{1,0:T(8,128)} %reduce-scatter.9.cloned.1.call-done) | copy-start | bytes 442372
  225.6 96.6 %copy-start.3 = (f32[16,2304]{1,0:T(8,128)S(1)}, f32[16,2304]{1,0:T(8,128)}, u32[]{:S(2)}) copy-start(f32[16,2304]{1,0:T(8,128)} %reduce-scatter.11.cloned.1.call-done) | copy-start | bytes 442372
  227.1 194.4 %reduce-scatter.21.cloned.1.call-start = ((), (), s32[]{:S(2)}) async-start(), calls=%async_computation.14 | async-start | bytes 737280 | tf_op jit(solution)/shard_map/reduce_scatter | solution.py:52
  400.0 89.4 %reduce-scatter.23.cloned.1.call-start = ((), (), s32[]{:S(2)}) async-start(), calls=%async_computation.15 | async-start | bytes 1327104 | tf_op jit(solution)/shard_map/reduce_scatter | solution.py:53
  413.4 118.2 %copy-start.6 = (f32[16,2304]{1,0:T(8,128)}, f32[16,2304]{1,0:T(8,128)S(1)}, u32[]{:S(2)}) copy-start(f32[16,2304]{1,0:T(8,128)S(1)} %get-tuple-element.18) | copy-start | bytes 442372
Sparse Core Ops, SparseCore 0:
  47.2 23.1 reduce-scatter.8
  73.8 64.0 reduce-scatter.10
  140.4 21.0 reduce-scatter.16
  164.8 65.3 reduce-scatter.18
  232.5 21.0 reduce-scatter.12
  256.8 64.0 reduce-scatter.14
  400.1 21.3 reduce-scatter.20
  424.9 64.4 reduce-scatter.22
where the time goes:
time: 539 us; the launch traced here: 538 us
  blocking collectives  275 us (51%)
  waiting for transfers between devices  203 us (38%)
  matrix products  21.6 us (4%)
  local copies, waits for them, and re-layouts  17.6 us (3%)
  between operations  15.2 us (3%)
  other arithmetic  5.91 us (1%)
    reduce_scatter x4, waiting for transfers between devices, apply_operator(): lax.psum_scatter(trans_sum, 'row', scatter_dimension=1, tiled=True)  173 us
    all_gather x4, blocking collectives, apply_operator(): col_vec = lax.all_gather(vec_bf, 'row', axis=1, tiled=True)  130 us
    psum x3, blocking collectives, quotients(): lax.psum((jnp.sum(block * image, axis=1), jnp.sum(block * block, axis=1))...  120 us
    reduce_scatter x4, waiting for transfers between devices, apply_operator(): lax.psum_scatter(direct_sum, 'col', scatter_dimension=1, tiled=True)  30.2 us
    all_gather x4, blocking collectives, apply_operator(): row_vec = lax.all_gather(vec_bf, 'col', axis=1, tiled=True)  25.1 us
  transfers between devices with their start and end apart: 8, of which 6 were waited for; matrix products, arithmetic and copies ran while one was open for 5% of the time, Pallas kernels for 0%

commit v1 on v0

v1 whole, which is shorter than its diff:
```python
import functools

import jax
import jax.numpy as jnp
from jax import lax
from jax.experimental import pallas as pl
from jax.experimental.pallas import tpu as pltpu
from jax.sharding import PartitionSpec as P

ITERS = 2
BS = 128
GROUP = 9
F32 = jnp.float32
BF16 = jnp.bfloat16
HI = lax.Precision.HIGHEST
MESH = pl.DeviceIdType.MESH


def dot_t(left, right, precision=None):
    return lax.dot_general(
        left, right, (((1,), (1,)), ((), ())), precision=precision, preferred_element_type=F32
    )


def dot_n(left, right, precision=None):
    return lax.dot_general(
        left, right, (((1,), (0,)), ((), ())), precision=precision, preferred_element_type=F32
    )


def kernel(
    n_row, n_col, nb, k, slots,
    block_in, search_in, precond_in, diag_in, blocks, row_smem, col_smem, live_smem,
    row_ids, col_ids, coeffs,
    block_out, ritz_out,
    sent, row_g, col_g, row_b, col_b, terms, row_acc, col_acc, row_send, col_send,
    row_part, col_part, scal, row_scal, col_scal,
    row_ssem, row_rsem, col_ssem, col_rsem,
):
    r = lax.axis_index("row")
    c = lax.axis_index("col")
    rows = nb * k
    grows = GROUP * k

    barrier = pltpu.get_barrier_semaphore()
    for d in range(1, n_row):
        pl.semaphore_signal(barrier, inc=1, device_id=(lax.rem(r + d, n_row), c), device_id_type=MESH)
    for d in range(1, n_col):
        pl.semaphore_signal(barrier, inc=1, device_id=(r, lax.rem(c + d, n_col)), device_id_type=MESH)

    def row_copy(phase, d, src, dst):
        return pltpu.make_async_remote_copy(
            src_ref=src, dst_ref=dst, send_sem=row_ssem.at[phase, d], recv_sem=row_rsem.at[phase, d],
            device_id=(lax.rem(r + d, n_row), c), device_id_type=MESH,
        )

    def col_copy(phase, d, src, dst):
        return pltpu.make_async_remote_copy(
            src_ref=src, dst_ref=dst, send_sem=col_ssem.at[phase, d], recv_sem=col_rsem.at[phase, d],
            device_id=(r, lax.rem(c + d, n_col)), device_id_type=MESH,
        )

    def start_gather(phase, values):
        sent[phase] = values
        by_col = [
            col_copy(phase, d, sent.at[phase], row_g.at[phase, pl.ds(c * nb, nb)]) for d in range(1, n_col)
        ]
        by_row = [
            row_copy(phase, d, sent.at[phase], col_g.at[phase, pl.ds(r * nb, nb)]) for d in range(1, n_row)
        ]
        for copy in by_col + by_row:
            copy.start()
        row_g[phase, pl.ds(c * nb, nb)] = values
        col_g[phase, pl.ds(r * nb, nb)] = values
        return by_col, by_row

    def wait_all(copies):
        for copy in copies:
            copy.wait()

    live = live_smem[0, 0]

    def hot(ids, count):
        alive = lax.broadcasted_iota(jnp.int32, (count, slots), 1) < live
        same = lax.broadcasted_iota(jnp.int32, (count, slots), 0) == ids
        one = jnp.where(same & alive, 1.0, 0.0).astype(BF16)
        return jnp.concatenate([one, one], axis=1)

    def slot_products(phase, source, index, dot):
        def body(group, carry):
            for u in range(8):
                s = group * 8 + u
                terms[pl.ds(pl.multiple_of(s * k, k), k), :] = dot(source[phase, index[0, s]], blocks[s])
            return carry

        lax.fori_loop(0, slots // 8, body, 0)

    def slot_sums(hots, acc, count):
        for q in range(k):
            part = terms[pl.ds(q, slots, stride=k), :]
            high = part.astype(BF16)
            low = (part - high.astype(F32)).astype(BF16)
            acc[pl.ds(q, count, stride=k), :] = dot_n(hots, jnp.concatenate([high, low], axis=0))

    def send_parts(phase, acc, out, part, count, me, make):
        out[phase] = acc[...].astype(BF16).reshape(count * nb, k, BS)
        copies = [
            make(3 + phase, d, out.at[phase, pl.ds(lax.rem(me + d, count) * nb, nb)], part.at[phase, me])
            for d in range(1, count)
        ]
        for copy in copies:
            copy.start()
        part[phase, me] = out[phase, pl.ds(me * nb, nb)]
        return copies

    def part_sum(phase, part, count):
        total = part[phase, 0].astype(F32)
        for i in range(1, count):
            total = total + part[phase, i].astype(F32)
        return total

    def inner(gathered, acc, count):
        total = jnp.zeros((k, BS), F32)
        for i in range(0, count * nb, GROUP):
            total = total + jnp.sum(
                gathered(i).astype(F32) * acc[i * k : (i + GROUP) * k, :].reshape(GROUP, k, BS), axis=0
            )
        return total

    def local_dot(left, right):
        return jnp.sum(left * right, axis=0)

    lane = lax.broadcasted_iota(jnp.int32, (k, BS), 1)

    def reduce_row(phase, num, den):
        packed = jnp.where(
            lane < BS // 2, jnp.sum(num, axis=1, keepdims=True), jnp.sum(den, axis=1, keepdims=True)
        )
        scal[0, phase] = packed
        row_scal[phase, r] = packed
        copies = [row_copy(5 + phase, d, scal.at[0, phase], row_scal.at[phase, r]) for d in range(1, n_row)]
        for copy in copies:
            copy.start()
        return copies

    def reduce_col(phase, copies):
        wait_all(copies)
        packed = jnp.sum(row_scal[phase], axis=0)
        scal[1, phase] = packed
        col_scal[phase, c] = packed
        copies = [col_copy(5 + phase, d, scal.at[1, phase], col_scal.at[phase, c]) for d in range(1, n_col)]
        for copy in copies:
            copy.start()
        wait_all(copies)
        total = jnp.sum(col_scal[phase], axis=0)
        return total[:, 0:1] / total[:, BS // 2 : BS // 2 + 1]

    def tiles(flat):
        return jnp.stack([flat[:, j * BS : (j + 1) * BS] for j in range(nb)], axis=0)

    start = block_in[...]
    block = tiles(start)
    pl.semaphore_wait(barrier, n_row + n_col - 2)
    by_col, by_row = start_gather(0, block.astype(BF16))

    search = tiles(search_in[...])
    precond = precond_in[...].reshape(nb, 1, BS)
    diag = diag_in[...].reshape(nb, 1, BS)
    hot_rows = hot(row_ids[...], n_col * nb)
    hot_cols = hot(col_ids[...], n_row * nb)

    spread = (
        lax.broadcasted_iota(jnp.int32, (grows, k), 0) % k == lax.broadcasted_iota(jnp.int32, (grows, k), 1)
    ).astype(F32)
    same_group = (
        lax.broadcasted_iota(jnp.int32, (grows, grows), 0) // k
        == lax.broadcasted_iota(jnp.int32, (grows, grows), 1) // k
    )

    def expand(coef):
        wide = dot_t(dot_t(spread, coef, HI), spread, HI)
        return jnp.where(same_group, wide, 0.0)

    mats = [[expand(coeffs[i, j]) for j in range(3)] for i in range(ITERS)]

    def combine(mat, values):
        flat = values.reshape(rows, BS)
        return jnp.concatenate(
            [dot_n(mat, flat[i : i + grows], HI) for i in range(0, rows, grows)], axis=0
        ).reshape(nb, k, BS)

    def combine_gathered(mat, values):
        high = mat.astype(BF16)
        low = (mat - high.astype(F32)).astype(BF16)
        flat = values.reshape(grows, BS)
        return (dot_n(high, flat) + dot_n(low, flat)).reshape(GROUP, k, BS)

    def operator(phase, by_col, by_row, send):
        wait_all(by_col)
        slot_products(phase, row_g, row_smem, dot_n)
        slot_sums(hot_cols, col_acc, n_row * nb)
        row_parts = send_parts(phase, col_acc, col_send, col_part, n_row, r, row_copy) if send else []
        wait_all(by_row)
        slot_products(phase, col_g, col_smem, dot_t)
        slot_sums(hot_rows, row_acc, n_col * nb)
        col_parts = send_parts(phase, row_acc, row_send, row_part, n_col, c, col_copy) if send else []
        return row_parts + col_parts

    parts = operator(0, by_col, by_row, True)
    own = diag * sent[0].astype(F32)
    num = (
        local_dot(block, own)
        + inner(lambda i: row_g[0, i : i + GROUP], row_acc, n_col)
        + inner(lambda i: col_g[0, i : i + GROUP], col_acc, n_row)
    )
    copies = reduce_row(0, num, local_dot(block, block))
    ritz = reduce_col(0, copies)
    wait_all(parts)
    image = own + part_sum(0, row_part, n_col) + part_sum(0, col_part, n_row)

    for i in range(ITERS):
        mat_x, mat_w, mat_p = mats[i]
        phase = i + 1
        residual = (image - ritz[None] * block) * precond
        search = combine(mat_w, residual) + combine(mat_p, search)
        by_col, by_row = start_gather(phase, search.astype(BF16))
        block = combine(mat_x, block) + search
        own = diag * sent[phase].astype(F32)
        image = combine(mat_x, image) + own
        num = local_dot(block, image)
        den = local_dot(block, block)
        for gathered, total, count in ((row_g, row_b, n_col), (col_g, col_b, n_row)):
            for g in range(0, count * nb, GROUP):
                old = gathered[0, g : g + GROUP] if i == 0 else total[g : g + GROUP]
                total[g : g + GROUP] = combine_gathered(mat_x, old).astype(BF16)
        if i == ITERS - 1:
            for j in range(nb):
                block_out[:, j * BS : (j + 1) * BS] = block[j]
        parts = operator(phase, by_col, by_row, i < ITERS - 1)
        for gathered, total, count in ((row_g, row_b, n_col), (col_g, col_b, n_row)):
            for g in range(0, count * nb, GROUP):
                total[g : g + GROUP] = (
                    total[g : g + GROUP].astype(F32) + gathered[phase, g : g + GROUP].astype(F32)
                ).astype(BF16)
        num = (
            num
            + inner(lambda g: row_b[g : g + GROUP], row_acc, n_col)
            + inner(lambda g: col_b[g : g + GROUP], col_acc, n_row)
        )
        copies = reduce_row(phase, num, den)
        ritz = reduce_col(phase, copies)
        if i < ITERS - 1:
            wait_all(parts)
            image = image + part_sum(phase, row_part, n_col) + part_sum(phase, col_part, n_row)

    ritz_out[...] = jnp.broadcast_to(ritz, (k, BS))


def on_device(
    n_row, n_col, start_block, start_search, precond, diag_energy, blocks, row_index, col_index,
    live_count, ritz_coeffs,
):
    k, length = start_block.shape
    nb = length // BS
    slots = blocks.shape[2]
    phases = ITERS + 1
    vmem = pl.BlockSpec(memory_space=pltpu.VMEM)
    smem = pl.BlockSpec(memory_space=pltpu.SMEM)
    row_ids = row_index[0]
    col_ids = col_index[0]
    block, ritz = pl.pallas_call(
        functools.partial(kernel, n_row, n_col, nb, k, slots),
        out_shape=(
            jax.ShapeDtypeStruct((k, length), F32),
            jax.ShapeDtypeStruct((k, BS), F32),
        ),
        in_specs=[vmem] * 5 + [smem] * 3 + [vmem] * 3,
        out_specs=(vmem, vmem),
        scratch_shapes=[
            pltpu.VMEM((phases, nb, k, BS), BF16),
            pltpu.VMEM((phases, n_col * nb, k, BS), BF16),
            pltpu.VMEM((phases, n_row * nb, k, BS), BF16),
            pltpu.VMEM((n_col * nb, k, BS), BF16),
            pltpu.VMEM((n_row * nb, k, BS), BF16),
            pltpu.VMEM((slots * k, BS), F32),
            pltpu.VMEM((n_col * nb * k, BS), F32),
            pltpu.VMEM((n_row * nb * k, BS), F32),
            pltpu.VMEM((phases - 1, n_col * nb, k, BS), BF16),
            pltpu.VMEM((phases - 1, n_row * nb, k, BS), BF16),
            pltpu.VMEM((phases - 1, n_col, nb, k, BS), BF16),
            pltpu.VMEM((phases - 1, n_row, nb, k, BS), BF16),
            pltpu.VMEM((2, phases, k, BS), F32),
            pltpu.VMEM((phases, n_row, k, BS), F32),
            pltpu.VMEM((phases, n_col, k, BS), F32),
            pltpu.SemaphoreType.DMA((8, n_row)),
            pltpu.SemaphoreType.DMA((8, n_row)),
            pltpu.SemaphoreType.DMA((8, n_col)),
            pltpu.SemaphoreType.DMA((8, n_col)),
        ],
        compiler_params=pltpu.CompilerParams(
            collective_id=0, has_side_effects=True, vmem_limit_bytes=48 * 1024 * 1024
        ),
    )(
        start_block, start_search, precond.reshape(nb, BS), diag_energy.reshape(nb, BS), blocks[0, 0],
        row_ids, col_ids, live_count, row_ids, col_ids, ritz_coeffs,
    )
    return block, ritz[:, 0]


def solution(mesh):
    placed = (
        P(None, ("row", "col")),
        P(None, ("row", "col")),
        P(("row", "col")),
        P(("row", "col")),
        P("row", "col", None, None, None),
        P("row", "col", None),
        P("row", "col", None),
        P("row", "col"),
        P(),
    )
    return jax.shard_map(
        functools.partial(on_device, mesh.shape["row"], mesh.shape["col"]),
        mesh=mesh,
        in_specs=placed,
        out_specs=(P(None, ("row", "col")), P()),
        check_vma=False,
    )
```

time: 539 us -> 108 us (0.20)
  blocking collectives: 275 us -> 0 us
  waiting for transfers between devices: 203 us -> 0 us
  Pallas kernels: 0 us -> 98.3 us
  matrix products: 21.6 us -> 0 us
  between operations: 15.2 us -> 1.3 us
  local copies, waits for them, and re-layouts: 17.6 us -> 8.21 us
  other arithmetic: 5.91 us -> 0 us
    reduce_scatter x8 -> x0, waiting for transfers between devices: 203 us -> none  [the longest x4 173 us: apply_operator(): lax.psum_scatter(trans_sum, 'row', scatter_dimension=1, tiled=True)]
    all_gather x8 -> x0, blocking collectives: 155 us -> none  [the longest x4 130 us: apply_operator(): col_vec = lax.all_gather(vec_bf, 'row', axis=1, tiled=True)]
    psum x3 -> x0, blocking collectives: 120 us -> none  [quotients(): lax.psum((jnp.sum(block * image, axis=1), jnp.sum(block * block, axis=1))...]
    pallas_call x0 -> x1, Pallas kernels: none -> 98.3 us  [on_device(): pl.pallas_call(functools.partial(kernel, n_row, n_col, nb, k, slots), out...]
    dot_general x28 -> x0, matrix products: 21.6 us -> none  [the longest x4 4.9 us: slot_terms(): jnp.einsum('bij,bkj->bki', tile_set, gathered_col, preferred_element_type...]
    gather x8 -> x0, local copies, waits for them, and re-layouts: 6.81 us -> none  [the longest x4 3.6 us: slot_terms(): gathered_col = jnp.take(col_tiles, col_ids, axis=0)]
  transfers between devices with their start and end apart: 8 -> 0, of which waited for: 6 -> 0; matrix products, arithmetic and copies ran while one was open for 5% -> 0% of each run, Pallas kernels for 0% -> 0%
where the time goes in v1:
time: 108 us
  Pallas kernels  98.3 us (91%)
  local copies, waits for them, and re-layouts  8.21 us (8%)
  between operations  1.3 us (1%)
    pallas_call x1, Pallas kernels, on_device(): pl.pallas_call(functools.partial(kernel, n_row, n_col, nb, k, slots), out...  98.3 us
    unnamed x17, local copies, waits for them, and re-layouts  7.58 us

profile of v1, /device:TPU:0, one launch (start us, length us, event | category | flops | bytes accessed | tf_op | source)
XLA Modules:
  0.0 107.8 jit_solution(147549897654169929)
XLA Ops:
  1.3 0.0 copy-start
  1.3 1.6 %copy-done = bf16[1,1,64,128,128]{4,3,2,1,0:T(8,128)(2,1)S(1)} copy-done((bf16[1,1,64,128,128]{4,3,2,1,0:T(8,128)(2,1)S(1)}, bf16[1,1,64,128,128]{4,3,2,1,0:T(8,128)(2,1)}, u32[]{:S(2)}) %copy-start) | copy-done | bytes 2097176
  2.9 0.0 copy-start.1
  2.9 0.9 copy-done.1
  3.8 0.0 copy-start.2
  3.8 0.9 copy-done.2
  4.7 0.0 copy-start.3
  4.7 0.8 copy-done.3
  5.5 0.0 copy-start.4
  5.5 0.7 copy-done.4
  6.2 0.0 copy-start.5
  6.2 0.7 copy-done.5
  6.9 0.0 copy-start.6
  6.9 0.7 copy-done.6
  7.6 0.0 copy-start.7
  7.6 0.7 copy-done.7
  8.2 98.3 %shard_map.104 = (f32[16,2304]{1,0:T(8,128)S(1)}, f32[16,128]{1,0:T(8,128)S(1)}) custom-call(f32[16,2304]{1,0:T(8,128)S(1)} %copy-done.1, f32[16,2304]{1,0:T(8,128)S(1)} %copy-done.2, f32[18,128]{1,0:T(8,128)S(1)} %bitcast.6, f32[18,128]{1,0:T(8,128)S(1)} %bitcast.7, bf16[64,128,128]{2,1,0:T(8,128)(2,1)S(1)} %bitcast.5, s32[1,64]{1,0:T(1,128)S(1)} %bitcast.8, ...), custom_call_target="tpu_custom_call" | custom-call | tf_op jit(solution)/shard_map/pallas_call | solution.py:271
  106.5 0.6 slice_reduce_fusion
  107.2 0.7 copy.13
Async XLA Ops:
  1.3 1.6 %copy-start = (bf16[1,1,64,128,128]{4,3,2,1,0:T(8,128)(2,1)S(1)}, bf16[1,1,64,128,128]{4,3,2,1,0:T(8,128)(2,1)}, u32[]{:S(2)}) copy-start(bf16[1,1,64,128,128]{4,3,2,1,0:T(8,128)(2,1)} %param.13) | copy-start | bytes 6291460
  2.9 0.9 copy-start.1
  3.8 0.9 copy-start.2
  4.7 0.8 copy-start.3
  5.5 0.7 copy-start.4
  6.2 0.7 copy-start.5
  6.9 0.7 copy-start.6
  7.6 0.7 copy-start.7

commit v2 on v1

--- a/solution.py
+++ b/solution.py
@@ -30,15 +30,29 @@
 
 def kernel(
     n_row, n_col, nb, k, slots,
-    block_in, search_in, precond_in, diag_in, blocks, row_smem, col_smem, live_smem,
-    row_ids, col_ids, coeffs,
+    block_hbm, search_hbm, precond_hbm, diag_hbm, blocks_hbm, row_ids_hbm, col_ids_hbm, coeffs_hbm,
+    row_smem, col_smem, live_smem,
     block_out, ritz_out,
     sent, row_g, col_g, row_b, col_b, terms, row_acc, col_acc, row_send, col_send,
     row_part, col_part, scal, row_scal, col_scal,
-    row_ssem, row_rsem, col_ssem, col_rsem,
+    x_part, z_send, row_ssem, row_rsem, col_ssem, col_rsem,
+    block_in, search_in, precond_in, diag_in, blocks, row_ids, col_ids, coeffs, load_sem,
 ):
+    loads = [
+        pltpu.make_async_copy(src, dst, load_sem.at[i])
+        for i, (src, dst) in enumerate((
+            (block_hbm, block_in), (search_hbm, search_in), (precond_hbm, precond_in),
+            (diag_hbm, diag_in), (blocks_hbm, blocks), (row_ids_hbm, row_ids),
+            (col_ids_hbm, col_ids), (coeffs_hbm, coeffs),
+        ))
+    ]
+    for load in loads:
+        load.start()
     r = lax.axis_index("row")
     c = lax.axis_index("col")
+    n_z = n_row // 2
+    z = r // 2
+    x = lax.rem(r, 2)
     rows = nb * k
     grows = GROUP * k
 
@@ -60,19 +74,42 @@
             device_id=(r, lax.rem(c + d, n_col)), device_id_type=MESH,
         )
 
+    def x_copy(phase, sem, src, dst):
+        return pltpu.make_async_remote_copy(
+            src_ref=src, dst_ref=dst, send_sem=row_ssem.at[phase, sem], recv_sem=row_rsem.at[phase, sem],
+            device_id=(z * 2 + 1 - x, c), device_id_type=MESH,
+        )
+
+    def z_copy(phase, d, sem, src, dst):
+        return pltpu.make_async_remote_copy(
+            src_ref=src, dst_ref=dst, send_sem=row_ssem.at[phase, sem], recv_sem=row_rsem.at[phase, sem],
+            device_id=(lax.rem(z + d, n_z) * 2 + x, c), device_id_type=MESH,
+        )
+
     def start_gather(phase, values):
         sent[phase] = values
         by_col = [
             col_copy(phase, d, sent.at[phase], row_g.at[phase, pl.ds(c * nb, nb)]) for d in range(1, n_col)
         ]
-        by_row = [
-            row_copy(phase, d, sent.at[phase], col_g.at[phase, pl.ds(r * nb, nb)]) for d in range(1, n_row)
-        ]
-        for copy in by_col + by_row:
+        own = col_g.at[phase, pl.ds(r * nb, nb)]
+        by_z = [z_copy(phase, d, d, sent.at[phase], own) for d in range(1, n_z)]
+        by_x = [x_copy(phase, n_z, sent.at[phase], own)]
+        for copy in by_z + by_x + by_col:
             copy.start()
         row_g[phase, pl.ds(c * nb, nb)] = values
         col_g[phase, pl.ds(r * nb, nb)] = values
-        return by_col, by_row
+        return by_col, by_z, by_x
+
+    def forward(phase, by_z):
+        by_x = []
+        for d in range(1, n_z):
+            by_z[d - 1].wait_recv()
+            piece = col_g.at[phase, pl.ds((lax.rem(z - d + n_z, n_z) * 2 + x) * nb, nb)]
+            by_x.append(x_copy(phase, n_z + d, piece, piece))
+            by_x[-1].start()
+        for copy in by_z:
+            copy.wait_send()
+        return by_x
 
     def wait_all(copies):
         for copy in copies:
@@ -111,6 +148,32 @@
         for copy in copies:
             copy.start()
         part[phase, me] = out[phase, pl.ds(me * nb, nb)]
+        return copies
+
+    order = list(range(1, n_z)) + [0]
+
+    def send_x(phase):
+        col_send[phase] = col_acc[...].astype(BF16).reshape(n_row * nb, k, BS)
+        copies = {}
+        for d in order:
+            there = (lax.rem(z + d, n_z) * 2 + 1 - x) * nb
+            copies[d] = x_copy(3 + phase, d, col_send.at[phase, pl.ds(there, nb)], x_part.at[phase, d])
+            copies[d].start()
+        return copies
+
+    def send_z(phase, by_x):
+        copies = []
+        for d in order:
+            by_x[d].wait()
+            here = (lax.rem(z + d, n_z) * 2 + x) * rows
+            mine = col_acc[pl.ds(pl.multiple_of(here, rows), rows), :].reshape(nb, k, BS)
+            both = (mine + x_part[phase, d].astype(F32)).astype(BF16)
+            if d == 0:
+                col_part[phase, 0] = both
+            else:
+                z_send[phase, d] = both
+                copies.append(z_copy(3 + phase, d, n_z + d, z_send.at[phase, d], col_part.at[phase, d]))
+                copies[-1].start()
         return copies
 
     def part_sum(phase, part, count):
@@ -158,10 +221,13 @@
     def tiles(flat):
         return jnp.stack([flat[:, j * BS : (j + 1) * BS] for j in range(nb)], axis=0)
 
+    loads[0].wait()
     start = block_in[...]
     block = tiles(start)
     pl.semaphore_wait(barrier, n_row + n_col - 2)
-    by_col, by_row = start_gather(0, block.astype(BF16))
+    by_col, by_z, by_x = start_gather(0, block.astype(BF16))
+    for load in loads[1:]:
+        load.wait()
 
     search = tiles(search_in[...])
     precond = precond_in[...].reshape(nb, 1, BS)
@@ -195,18 +261,19 @@
         flat = values.reshape(grows, BS)
         return (dot_n(high, flat) + dot_n(low, flat)).reshape(GROUP, k, BS)
 
-    def operator(phase, by_col, by_row, send):
+    def operator(phase, by_col, by_z, by_x, send):
+        by_x = by_x + forward(phase, by_z)
         wait_all(by_col)
         slot_products(phase, row_g, row_smem, dot_n)
         slot_sums(hot_cols, col_acc, n_row * nb)
-        row_parts = send_parts(phase, col_acc, col_send, col_part, n_row, r, row_copy) if send else []
-        wait_all(by_row)
+        row_parts = send_x(phase) if send else {}
+        wait_all(by_x)
         slot_products(phase, col_g, col_smem, dot_t)
         slot_sums(hot_rows, row_acc, n_col * nb)
         col_parts = send_parts(phase, row_acc, row_send, row_part, n_col, c, col_copy) if send else []
-        return row_parts + col_parts
-
-    parts = operator(0, by_col, by_row, True)
+        return row_parts, col_parts
+
+    row_parts, col_parts = operator(0, by_col, by_z, by_x, True)
     own = diag * sent[0].astype(F32)
     num = (
         local_dot(block, own)
@@ -214,16 +281,17 @@
         + inner(lambda i: col_g[0, i : i + GROUP], col_acc, n_row)
     )
     copies = reduce_row(0, num, local_dot(block, block))
+    parts = send_z(0, row_parts) + col_parts
     ritz = reduce_col(0, copies)
     wait_all(parts)
-    image = own + part_sum(0, row_part, n_col) + part_sum(0, col_part, n_row)
+    image = own + part_sum(0, row_part, n_col) + part_sum(0, col_part, n_z)
 
     for i in range(ITERS):
         mat_x, mat_w, mat_p = mats[i]
         phase = i + 1
         residual = (image - ritz[None] * block) * precond
         search = combine(mat_w, residual) + combine(mat_p, search)
-        by_col, by_row = start_gather(phase, search.astype(BF16))
+        by_col, by_z, by_x = start_gather(phase, search.astype(BF16))
         block = combine(mat_x, block) + search
         own = diag * sent[phase].astype(F32)
         image = combine(mat_x, image) + own
@@ -236,7 +304,7 @@
         if i == ITERS - 1:
             for j in range(nb):
                 block_out[:, j * BS : (j + 1) * BS] = block[j]
-        parts = operator(phase, by_col, by_row, i < ITERS - 1)
+        row_parts, col_parts = operator(phase, by_col, by_z, by_x, i < ITERS - 1)
         for gathered, total, count in ((row_g, row_b, n_col), (col_g, col_b, n_row)):
             for g in range(0, count * nb, GROUP):
                 total[g : g + GROUP] = (
@@ -248,10 +316,11 @@
             + inner(lambda g: col_b[g : g + GROUP], col_acc, n_row)
         )
         copies = reduce_row(phase, num, den)
+        parts = send_z(phase, row_parts) + col_parts if i < ITERS - 1 else []
         ritz = reduce_col(phase, copies)
         if i < ITERS - 1:
             wait_all(parts)
-            image = image + part_sum(phase, row_part, n_col) + part_sum(phase, col_part, n_row)
+            image = image + part_sum(phase, row_part, n_col) + part_sum(phase, col_part, n_z)
 
     ritz_out[...] = jnp.broadcast_to(ritz, (k, BS))
 
@@ -265,6 +334,7 @@
     slots = blocks.shape[2]
     phases = ITERS + 1
     vmem = pl.BlockSpec(memory_space=pltpu.VMEM)
+    hbm = pl.BlockSpec(memory_space=pltpu.HBM)
     smem = pl.BlockSpec(memory_space=pltpu.SMEM)
     row_ids = row_index[0]
     col_ids = col_index[0]
@@ -274,7 +344,7 @@
             jax.ShapeDtypeStruct((k, length), F32),
             jax.ShapeDtypeStruct((k, BS), F32),
         ),
-        in_specs=[vmem] * 5 + [smem] * 3 + [vmem] * 3,
+        in_specs=[hbm] * 8 + [smem] * 3,
         out_specs=(vmem, vmem),
         scratch_shapes=[
             pltpu.VMEM((phases, nb, k, BS), BF16),
@@ -288,21 +358,32 @@
             pltpu.VMEM((phases - 1, n_col * nb, k, BS), BF16),
             pltpu.VMEM((phases - 1, n_row * nb, k, BS), BF16),
             pltpu.VMEM((phases - 1, n_col, nb, k, BS), BF16),
-            pltpu.VMEM((phases - 1, n_row, nb, k, BS), BF16),
+            pltpu.VMEM((phases - 1, n_row // 2, nb, k, BS), BF16),
             pltpu.VMEM((2, phases, k, BS), F32),
             pltpu.VMEM((phases, n_row, k, BS), F32),
             pltpu.VMEM((phases, n_col, k, BS), F32),
+            pltpu.VMEM((phases - 1, n_row // 2, nb, k, BS), BF16),
+            pltpu.VMEM((phases - 1, n_row // 2, nb, k, BS), BF16),
             pltpu.SemaphoreType.DMA((8, n_row)),
             pltpu.SemaphoreType.DMA((8, n_row)),
             pltpu.SemaphoreType.DMA((8, n_col)),
             pltpu.SemaphoreType.DMA((8, n_col)),
+            pltpu.VMEM((k, length), F32),
+            pltpu.VMEM((k, length), F32),
+            pltpu.VMEM((nb, BS), F32),
+            pltpu.VMEM((nb, BS), F32),
+            pltpu.VMEM((slots, BS, BS), BF16),
+            pltpu.VMEM((1, slots), jnp.int32),
+            pltpu.VMEM((1, slots), jnp.int32),
+            pltpu.VMEM(ritz_coeffs.shape, F32),
+            pltpu.SemaphoreType.DMA((8,)),
         ],
         compiler_params=pltpu.CompilerParams(
             collective_id=0, has_side_effects=True, vmem_limit_bytes=48 * 1024 * 1024
         ),
     )(
         start_block, start_search, precond.reshape(nb, BS), diag_energy.reshape(nb, BS), blocks[0, 0],
-        row_ids, col_ids, live_count, row_ids, col_ids, ritz_coeffs,
+        row_ids, col_ids, ritz_coeffs, row_ids, col_ids, live_count,
     )
     return block, ritz[:, 0]
 

time: 108 us -> 90.2 us (0.84)
  Pallas kernels: 98.3 us -> 80.3 us
    pallas_call x1, Pallas kernels: 98.3 us -> 80.3 us  [on_device(): pl.pallas_call(functools.partial(kernel, n_row, n_col, nb, k, slots), out...]
where the time goes in v2:
time: 90.2 us; the launch traced here: 89.9 us
  Pallas kernels  80.3 us (89%)
  local copies, waits for them, and re-layouts  8.21 us (9%)
  between operations  1.3 us (1%)
    pallas_call x1, Pallas kernels, on_device(): pl.pallas_call(functools.partial(kernel, n_row, n_col, nb, k, slots), out...  80.3 us
    unnamed x17, local copies, waits for them, and re-layouts  7.58 us

profile of v2, /device:TPU:0, one launch (start us, length us, event | category | flops | bytes accessed | tf_op | source)
XLA Modules:
  0.0 89.9 jit_solution(9674660095551217357)
XLA Ops:
  1.3 0.0 copy-start
  1.3 1.6 %copy-done = bf16[1,1,64,128,128]{4,3,2,1,0:T(8,128)(2,1)S(1)} copy-done((bf16[1,1,64,128,128]{4,3,2,1,0:T(8,128)(2,1)S(1)}, bf16[1,1,64,128,128]{4,3,2,1,0:T(8,128)(2,1)}, u32[]{:S(2)}) %copy-start) | copy-done | bytes 2097176
  2.9 0.0 copy-start.1
  2.9 0.9 %copy-done.1 = f32[16,2304]{1,0:T(8,128)S(1)} copy-done((f32[16,2304]{1,0:T(8,128)S(1)}, f32[16,2304]{1,0:T(8,128)}, u32[]{:S(2)}) %copy-start.1) | copy-done | bytes 147480
  3.8 0.0 copy-start.2
  3.8 0.9 %copy-done.2 = f32[16,2304]{1,0:T(8,128)S(1)} copy-done((f32[16,2304]{1,0:T(8,128)S(1)}, f32[16,2304]{1,0:T(8,128)}, u32[]{:S(2)}) %copy-start.2) | copy-done | bytes 147480
  4.7 0.0 copy-start.3
  4.7 0.8 copy-done.3
  5.5 0.0 copy-start.4
  5.5 0.7 copy-done.4
  6.2 0.0 copy-start.5
  6.2 0.7 copy-done.5
  6.9 0.0 copy-start.6
  6.9 0.7 copy-done.6
  7.6 0.0 copy-start.7
  7.6 0.7 copy-done.7
  8.2 80.3 %shard_map.104 = (f32[16,2304]{1,0:T(8,128)S(1)}, f32[16,128]{1,0:T(8,128)S(1)}) custom-call(f32[16,2304]{1,0:T(8,128)S(1)} %copy-done.1, f32[16,2304]{1,0:T(8,128)S(1)} %copy-done.2, f32[18,128]{1,0:T(8,128)S(1)} %bitcast.6, f32[18,128]{1,0:T(8,128)S(1)} %bitcast.7, bf16[64,128,128]{2,1,0:T(8,128)(2,1)S(1)} %bitcast.5, s32[1,64]{1,0:T(1,128)S(1)} %bitcast.8, ...), custom_call_target="tpu_custom_call" | custom-call | tf_op jit(solution)/shard_map/pallas_call | solution.py:341
  88.6 0.6 slice_reduce_fusion
  89.2 0.7 copy.13
Async XLA Ops:
  1.3 1.6 %copy-start = (bf16[1,1,64,128,128]{4,3,2,1,0:T(8,128)(2,1)S(1)}, bf16[1,1,64,128,128]{4,3,2,1,0:T(8,128)(2,1)}, u32[]{:S(2)}) copy-start(bf16[1,1,64,128,128]{4,3,2,1,0:T(8,128)(2,1)} %param.13) | copy-start | bytes 6291460
  2.9 0.9 %copy-start.1 = (f32[16,2304]{1,0:T(8,128)S(1)}, f32[16,2304]{1,0:T(8,128)}, u32[]{:S(2)}) copy-start(f32[16,2304]{1,0:T(8,128)} %block_hbm.1) | copy-start | bytes 442372
  3.8 0.9 %copy-start.2 = (f32[16,2304]{1,0:T(8,128)S(1)}, f32[16,2304]{1,0:T(8,128)}, u32[]{:S(2)}) copy-start(f32[16,2304]{1,0:T(8,128)} %search_hbm.1) | copy-start | bytes 442372
  4.7 0.8 copy-start.3
  5.5 0.7 copy-start.4
  6.2 0.7 copy-start.5
  6.9 0.7 copy-start.6
  7.6 0.7 copy-start.7

commit v3 on v2

--- a/solution.py
+++ b/solution.py
@@ -33,7 +33,7 @@
     block_hbm, search_hbm, precond_hbm, diag_hbm, blocks_hbm, row_ids_hbm, col_ids_hbm, coeffs_hbm,
     row_smem, col_smem, live_smem,
     block_out, ritz_out,
-    sent, row_g, col_g, row_b, col_b, terms, row_acc, col_acc, row_send, col_send,
+    sent, row_g0, row_g1, row_g2, col_g0, col_g1, col_g2, row_b, col_b, terms, row_acc, col_acc, row_send, col_send,
     row_part, col_part, scal, row_scal, col_scal,
     x_part, z_send, row_ssem, row_rsem, col_ssem, col_rsem,
     block_in, search_in, precond_in, diag_in, blocks, row_ids, col_ids, coeffs, load_sem,
@@ -50,6 +50,8 @@
         load.start()
     r = lax.axis_index("row")
     c = lax.axis_index("col")
+    row_g = (row_g0, row_g1, row_g2)
+    col_g = (col_g0, col_g1, col_g2)
     n_z = n_row // 2
     z = r // 2
     x = lax.rem(r, 2)
@@ -89,22 +91,22 @@
     def start_gather(phase, values):
         sent[phase] = values
         by_col = [
-            col_copy(phase, d, sent.at[phase], row_g.at[phase, pl.ds(c * nb, nb)]) for d in range(1, n_col)
+            col_copy(phase, d, sent.at[phase], row_g[phase].at[pl.ds(c * nb, nb)]) for d in range(1, n_col)
         ]
-        own = col_g.at[phase, pl.ds(r * nb, nb)]
+        own = col_g[phase].at[pl.ds(r * nb, nb)]
         by_z = [z_copy(phase, d, d, sent.at[phase], own) for d in range(1, n_z)]
         by_x = [x_copy(phase, n_z, sent.at[phase], own)]
         for copy in by_z + by_x + by_col:
             copy.start()
-        row_g[phase, pl.ds(c * nb, nb)] = values
-        col_g[phase, pl.ds(r * nb, nb)] = values
+        row_g[phase][pl.ds(c * nb, nb)] = values
+        col_g[phase][pl.ds(r * nb, nb)] = values
         return by_col, by_z, by_x
 
     def forward(phase, by_z):
         by_x = []
         for d in range(1, n_z):
             by_z[d - 1].wait_recv()
-            piece = col_g.at[phase, pl.ds((lax.rem(z - d + n_z, n_z) * 2 + x) * nb, nb)]
+            piece = col_g[phase].at[pl.ds((lax.rem(z - d + n_z, n_z) * 2 + x) * nb, nb)]
             by_x.append(x_copy(phase, n_z + d, piece, piece))
             by_x[-1].start()
         for copy in by_z:
@@ -127,7 +129,7 @@
         def body(group, carry):
             for u in range(8):
                 s = group * 8 + u
-                terms[pl.ds(pl.multiple_of(s * k, k), k), :] = dot(source[phase, index[0, s]], blocks[s])
+                terms[pl.ds(pl.multiple_of(s * k, k), k), :] = dot(source[phase][index[0, s]], blocks[s])
             return carry
 
         lax.fori_loop(0, slots // 8, body, 0)
@@ -261,26 +263,26 @@
         flat = values.reshape(grows, BS)
         return (dot_n(high, flat) + dot_n(low, flat)).reshape(GROUP, k, BS)
 
-    def operator(phase, by_col, by_z, by_x, send):
+    def operator(phase, by_col, by_z, by_x, send, early=None):
         by_x = by_x + forward(phase, by_z)
         wait_all(by_col)
         slot_products(phase, row_g, row_smem, dot_n)
         slot_sums(hot_cols, col_acc, n_row * nb)
         row_parts = send_x(phase) if send else {}
         wait_all(by_x)
+        early_copies = early() if early else []
         slot_products(phase, col_g, col_smem, dot_t)
         slot_sums(hot_rows, row_acc, n_col * nb)
         col_parts = send_parts(phase, row_acc, row_send, row_part, n_col, c, col_copy) if send else []
-        return row_parts, col_parts
-
-    row_parts, col_parts = operator(0, by_col, by_z, by_x, True)
+        return row_parts, col_parts, early_copies
+
     own = diag * sent[0].astype(F32)
-    num = (
-        local_dot(block, own)
-        + inner(lambda i: row_g[0, i : i + GROUP], row_acc, n_col)
-        + inner(lambda i: col_g[0, i : i + GROUP], col_acc, n_row)
-    )
-    copies = reduce_row(0, num, local_dot(block, block))
+
+    def early():
+        num = local_dot(block, own) + 2.0 * inner(lambda i: col_g[0][i : i + GROUP], col_acc, n_row)
+        return reduce_row(0, num, local_dot(block, block))
+
+    row_parts, col_parts, copies = operator(0, by_col, by_z, by_x, True, early)
     parts = send_z(0, row_parts) + col_parts
     ritz = reduce_col(0, copies)
     wait_all(parts)
@@ -299,16 +301,16 @@
         den = local_dot(block, block)
         for gathered, total, count in ((row_g, row_b, n_col), (col_g, col_b, n_row)):
             for g in range(0, count * nb, GROUP):
-                old = gathered[0, g : g + GROUP] if i == 0 else total[g : g + GROUP]
+                old = gathered[0][g : g + GROUP] if i == 0 else total[g : g + GROUP]
                 total[g : g + GROUP] = combine_gathered(mat_x, old).astype(BF16)
         if i == ITERS - 1:
             for j in range(nb):
                 block_out[:, j * BS : (j + 1) * BS] = block[j]
-        row_parts, col_parts = operator(phase, by_col, by_z, by_x, i < ITERS - 1)
+        row_parts, col_parts, _ = operator(phase, by_col, by_z, by_x, i < ITERS - 1)
         for gathered, total, count in ((row_g, row_b, n_col), (col_g, col_b, n_row)):
             for g in range(0, count * nb, GROUP):
                 total[g : g + GROUP] = (
-                    total[g : g + GROUP].astype(F32) + gathered[phase, g : g + GROUP].astype(F32)
+                    total[g : g + GROUP].astype(F32) + gathered[phase][g : g + GROUP].astype(F32)
                 ).astype(BF16)
         num = (
             num
@@ -348,8 +350,8 @@
         out_specs=(vmem, vmem),
         scratch_shapes=[
             pltpu.VMEM((phases, nb, k, BS), BF16),
-            pltpu.VMEM((phases, n_col * nb, k, BS), BF16),
-            pltpu.VMEM((phases, n_row * nb, k, BS), BF16),
+            *[pltpu.VMEM((n_col * nb, k, BS), BF16)] * phases,
+            *[pltpu.VMEM((n_row * nb, k, BS), BF16)] * phases,
             pltpu.VMEM((n_col * nb, k, BS), BF16),
             pltpu.VMEM((n_row * nb, k, BS), BF16),
             pltpu.VMEM((slots * k, BS), F32),

time: 90.2 us -> 88.1 us (0.977)
  Pallas kernels: 80.3 us -> 78.3 us
    pallas_call x1, Pallas kernels: 80.3 us -> 78.3 us  [on_device(): pl.pallas_call(functools.partial(kernel, n_row, n_col, nb, k, slots), out...]
where the time goes in v3:
time: 88.1 us; the launch traced here: 87.8 us
  Pallas kernels  78.3 us (89%)
  local copies, waits for them, and re-layouts  8.21 us (9%)
  between operations  1.3 us (1%)
    pallas_call x1, Pallas kernels, on_device(): pl.pallas_call(functools.partial(kernel, n_row, n_col, nb, k, slots), out...  78.3 us
    unnamed x17, local copies, waits for them, and re-layouts  7.58 us

profile of v3, /device:TPU:0, one launch (start us, length us, event | category | flops | bytes accessed | tf_op | source)
XLA Modules:
  0.0 87.8 jit_solution(18163737985612019233)
XLA Ops:
  1.3 0.0 copy-start
  1.3 1.6 %copy-done = bf16[1,1,64,128,128]{4,3,2,1,0:T(8,128)(2,1)S(1)} copy-done((bf16[1,1,64,128,128]{4,3,2,1,0:T(8,128)(2,1)S(1)}, bf16[1,1,64,128,128]{4,3,2,1,0:T(8,128)(2,1)}, u32[]{:S(2)}) %copy-start) | copy-done | bytes 2097176
  2.9 0.0 copy-start.1
  2.9 0.9 %copy-done.1 = f32[16,2304]{1,0:T(8,128)S(1)} copy-done((f32[16,2304]{1,0:T(8,128)S(1)}, f32[16,2304]{1,0:T(8,128)}, u32[]{:S(2)}) %copy-start.1) | copy-done | bytes 147480
  3.8 0.0 copy-start.2
  3.8 0.9 %copy-done.2 = f32[16,2304]{1,0:T(8,128)S(1)} copy-done((f32[16,2304]{1,0:T(8,128)S(1)}, f32[16,2304]{1,0:T(8,128)}, u32[]{:S(2)}) %copy-start.2) | copy-done | bytes 147480
  4.7 0.0 copy-start.3
  4.7 0.8 copy-done.3
  5.5 0.0 copy-start.4
  5.5 0.7 copy-done.4
  6.2 0.0 copy-start.5
  6.2 0.7 copy-done.5
  6.9 0.0 copy-start.6
  6.9 0.7 copy-done.6
  7.6 0.0 copy-start.7
  7.6 0.7 copy-done.7
  8.2 78.3 %shard_map.104 = (f32[16,2304]{1,0:T(8,128)S(1)}, f32[16,128]{1,0:T(8,128)S(1)}) custom-call(f32[16,2304]{1,0:T(8,128)S(1)} %copy-done.1, f32[16,2304]{1,0:T(8,128)S(1)} %copy-done.2, f32[18,128]{1,0:T(8,128)S(1)} %bitcast.6, f32[18,128]{1,0:T(8,128)S(1)} %bitcast.7, bf16[64,128,128]{2,1,0:T(8,128)(2,1)S(1)} %bitcast.5, s32[1,64]{1,0:T(1,128)S(1)} %bitcast.8, ...), custom_call_target="tpu_custom_call" | custom-call | tf_op jit(solution)/shard_map/pallas_call | solution.py:343
  86.5 0.6 slice_reduce_fusion
  87.1 0.7 copy.13
Async XLA Ops:
  1.3 1.6 %copy-start = (bf16[1,1,64,128,128]{4,3,2,1,0:T(8,128)(2,1)S(1)}, bf16[1,1,64,128,128]{4,3,2,1,0:T(8,128)(2,1)}, u32[]{:S(2)}) copy-start(bf16[1,1,64,128,128]{4,3,2,1,0:T(8,128)(2,1)} %param.13) | copy-start | bytes 6291460
  2.9 0.9 %copy-start.1 = (f32[16,2304]{1,0:T(8,128)S(1)}, f32[16,2304]{1,0:T(8,128)}, u32[]{:S(2)}) copy-start(f32[16,2304]{1,0:T(8,128)} %block_hbm.1) | copy-start | bytes 442372
  3.8 0.9 %copy-start.2 = (f32[16,2304]{1,0:T(8,128)S(1)}, f32[16,2304]{1,0:T(8,128)}, u32[]{:S(2)}) copy-start(f32[16,2304]{1,0:T(8,128)} %search_hbm.1) | copy-start | bytes 442372
  4.7 0.8 copy-start.3
  5.5 0.7 copy-start.4
  6.2 0.7 copy-start.5
  6.9 0.7 copy-start.6
  7.6 0.7 copy-start.7
